TPU v7x, 32 devices: a whole 2x2x4 slice. The times are simulated.
32 devices in a mesh: branch: 8 (over z, x), tensor: 4 (over y, core).
Axes of the slice: x: 2, y: 2, z: 4, core: 2. Of those that a mesh axis runs over, the one named last changes fastest.
Arguments:
- hidden: bfloat16 [1024, 4, 4096], P('branch', None, 'tensor'), may hold values from -6 to 6
- gain: float32 [4096], replicated, may hold values from 0.5 to 1.5
- w_query: bfloat16 [4096, 4096], P(None, 'tensor'), may hold values from -0.09375 to 0.09375
- w_keyval: bfloat16 [2, 4096, 1024], P(None, None, 'tensor'), may hold values from -0.09375 to 0.09375
- w_out: bfloat16 [4096, 4096], P('tensor'), may hold values from -0.09375 to 0.09375
- kv_codes: bfloat16 [256, 2, 64, 1024], P('branch', None, None, 'tensor'), may hold values from -12 to 12
- kv_scales: bfloat16 [256, 2, 8], P('branch', None, 'tensor'), may hold values from 0.5 to 24
- fork_export: int32 [64], P('branch'), may hold values from 0 to 31
- fork_pull: int32 [8, 64], replicated, may hold values from 0 to 63, as said below
- page_table: int32 [1024, 8], P('branch'), may hold values from 0 to 95
- lengths: int32 [1024], P('branch'), may hold values from 1 to 512, as said below
Outputs:
- mixed: bfloat16 [1024, 4, 4096], P('branch', None, 'tensor')
Inputs may be any that keep to these rules, and one draw needn't show every extreme that they name: `fork_pull`: an entry s * 8 + e names offered page e of group s. In each row at most 16 entries name one group, and some group is named exactly 16 times in every row. `lengths`: some branch has exactly 512 tokens.
All inputs are finite; a program needn't handle non-finite values.
Results may differ from a plain program's by a relative error of at most 0.017.
Values may be sent and summed in bfloat16 or wider, within the bound.
A program may use at most 128 MiB of HBM per device.

v0:
```python
import math

import jax
import jax.numpy as jnp
from jax import lax
from jax.sharding import PartitionSpec as P

HEADS = 32
KVH = 8
HD = 128


def rotate(values, positions):
    half = values.shape[-1] // 2
    freq = jnp.exp(
        -(2.0 * jnp.arange(half).astype(jnp.float32) / values.shape[-1]) * math.log(500000.0)
    )
    angle = positions.astype(jnp.float32)[:, None] * freq[None, :]
    cosine = jnp.cos(angle)[:, None, :]
    sine = jnp.sin(angle)[:, None, :]
    first = values[..., :half]
    second = values[..., half:]
    return jnp.concatenate(
        [first * cosine - second * sine, second * cosine + first * sine], axis=-1
    )


def attend_block(query, key_new, value_new, codes, scales, lengths_block):
    blocks, slots, page = (codes.shape[0], codes.shape[1], codes.shape[3])
    heads_here = query.shape[2]
    steps = query.shape[1]
    keys = codes[:, :, 0].reshape(blocks, slots, page, heads_here, HD)
    values = codes[:, :, 1].reshape(blocks, slots, page, heads_here, HD)
    key_scale = jnp.transpose(scales[:, :, 0].astype(jnp.float32), (0, 2, 1))[
        :, None, :, None, :, None
    ]
    value_scale = jnp.transpose(scales[:, :, 1].astype(jnp.float32), (0, 2, 1))[
        :, None, :, None, :, None
    ]
    context = (
        jnp.einsum("bthgd,bmphd->bthgmp", query, keys, preferred_element_type=jnp.float32)
        * key_scale
    )
    token = (
        jnp.arange(slots, dtype=jnp.int32)[:, None] * page
        + jnp.arange(page, dtype=jnp.int32)[None, :]
    )
    live = (token[None, :, :] < lengths_block[:, None, None])[:, None, None, None, :, :]
    fresh = jnp.einsum("bthgd,bshd->bthgs", query, key_new, preferred_element_type=jnp.float32)
    causal = (jnp.arange(steps)[:, None] >= jnp.arange(steps)[None, :])[None, :, None, None, :]
    context = jnp.where(live, context, -1e30)
    fresh = jnp.where(causal, fresh, -1e30)
    top = jnp.maximum(jnp.max(context, axis=(4, 5)), jnp.max(fresh, axis=4))
    context_exp = jnp.where(live, jnp.exp(context - top[..., None, None]), 0.0)
    fresh_exp = jnp.where(causal, jnp.exp(fresh - top[..., None]), 0.0)
    total = jnp.sum(context_exp, axis=(4, 5)) + jnp.sum(fresh_exp, axis=4)
    context_w = (context_exp / total[..., None, None] * value_scale).astype(jnp.bfloat16)
    fresh_w = (fresh_exp / total[..., None]).astype(jnp.bfloat16)
    result = jnp.einsum(
        "bthgmp,bmphd->bthgd", context_w, values, preferred_element_type=jnp.float32
    )
    result = result + jnp.einsum(
        "bthgs,bshd->bthgd", fresh_w, value_new, preferred_element_type=jnp.float32
    )
    return result.astype(jnp.bfloat16)


def per_device(
    hidden,
    gain,
    w_query,
    w_keyval,
    w_out,
    kv_codes,
    kv_scales,
    fork_export,
    fork_pull,
    page_table,
    lengths,
):
    full = lax.all_gather(hidden, "tensor", axis=2, tiled=True)
    branches, steps, width = full.shape
    rows = full.reshape(branches * steps, width).astype(jnp.float32)
    power = jnp.mean(rows * rows, axis=-1, keepdims=True)
    normed = (rows * lax.rsqrt(power + 1e-05) * gain).astype(jnp.bfloat16)
    heads_here = w_keyval.shape[-1] // HD
    group = HEADS // KVH
    positions = (lengths[:, None] + jnp.arange(steps, dtype=jnp.int32)[None, :]).reshape(-1)
    query = jnp.dot(normed, w_query, preferred_element_type=jnp.float32).reshape(
        -1, heads_here * group, HD
    )
    query = (
        (rotate(query, positions) * HD ** (-0.5))
        .astype(jnp.bfloat16)
        .reshape(branches, steps, heads_here, group, HD)
    )
    key_new = jnp.dot(normed, w_keyval[0], preferred_element_type=jnp.float32).reshape(
        -1, heads_here, HD
    )
    key_new = (
        rotate(key_new, positions).astype(jnp.bfloat16).reshape(branches, steps, heads_here, HD)
    )
    value_new = (
        jnp.dot(normed, w_keyval[1], preferred_element_type=jnp.float32)
        .astype(jnp.bfloat16)
        .reshape(branches, steps, heads_here, HD)
    )
    myself = lax.axis_index("branch")
    my_row = lax.dynamic_index_in_dim(fork_pull, myself, 0, keepdims=False)
    every_codes, every_scales = (
        lax.all_gather(kv_codes[fork_export], "branch", axis=0, tiled=True),
        lax.all_gather(kv_scales[fork_export], "branch", axis=0, tiled=True),
    )
    inherit_codes = every_codes[my_row]
    inherit_scales = every_scales[my_row]
    pool_codes = jnp.concatenate([inherit_codes, kv_codes], axis=0)
    pool_scales = jnp.concatenate([inherit_scales, kv_scales], axis=0)
    block = 8
    count = branches // block

    def shaped(array):
        return array.reshape((count, block) + array.shape[1:])

    def one_block(items):
        table, lens, query_b, key_b, value_b = items
        return attend_block(query_b, key_b, value_b, pool_codes[table], pool_scales[table], lens)

    attended = lax.map(
        one_block,
        (shaped(page_table), shaped(lengths), shaped(query), shaped(key_new), shaped(value_new)),
    )
    attended = attended.reshape(branches * steps, heads_here * group * HD)
    width_here = w_out.shape[1] // lax.axis_size("tensor")
    summed = lax.psum_scatter(
        lax.dot_general(
            w_out, attended, (((0,), (1,)), ((), ())), preferred_element_type=jnp.float32
        ).astype(jnp.bfloat16),
        "tensor",
        scatter_dimension=0,
        tiled=True,
    ).astype(jnp.float32)
    return summed.T.astype(jnp.bfloat16).reshape(branches, steps, width_here)


def solution(mesh):
    return jax.shard_map(
        per_device,
        mesh=mesh,
        in_specs=(
            P("branch", None, "tensor"),
            P(),
            P(None, "tensor"),
            P(None, None, "tensor"),
            P("tensor", None),
            P("branch", None, None, "tensor"),
            P("branch", None, "tensor"),
            P("branch"),
            P(),
            P("branch", None),
            P("branch"),
        ),
        out_specs=P("branch", None, "tensor"),
        check_vma=False,
    )
```

profile of v0, /device:TPU:0, one launch (start us, length us, event | category | flops | bytes accessed | tf_op | source)
XLA Modules:
  0.0 664.8 jit_solution(4150836456608211570)
XLA Ops:
  11.1 11.8 %copy.133 = bf16[1024,4096]{1,0:T(8,128)(2,1)} copy(bf16[1024,4096]{0,1:T(8,128)(2,1)} %bitcast.145) | data formatting | bytes 16777216 | tf_op jit(solution)/shard_map/dot_general | solution.py:89
  28.5 32.2 %all-gather.1 = bf16[64,2,2]{2,1,0:T(2,128)(2,1)S(1)} all-gather(bf16[8,2,2]{2,1,0:T(2,128)(2,1)S(1)} %gather_fusion.4), channel_id=3, replica_groups=mesh['branch'=8,'tensor'=4] {'branch'}, dimensions={0}, use_global_device_ids=true | all-gather | bytes 576 | tf_op jit(solution)/shard_map/all_gather | solution.py:112
  63.0 4.6 fusion.36
  67.6 5.1 fusion.38
  72.7 6.9 %reshape.324 = bf16[512,4096,1]{1,0,2:T(8,128)(2,1)} reshape(bf16[128,4,4096]{2,1,0:T(4,128)(2,1)} %fusion.38) | data formatting | bytes 8388608 | tf_op jit(solution)/shard_map/convert_element_type | solution.py:85
  79.6 6.9 %convert_element_type.76 = bf16[512,4096]{1,0:T(8,128)(2,1)} reshape(bf16[128,4,4096]{2,1,0:T(4,128)(2,1)} %fusion.38) | data formatting | bytes 8388608 | tf_op jit(solution)/shard_map/convert_element_type | solution.py:85
  86.5 8.3 %fusion.51 = f32[512,8,128]{0,2,1:T(8,128)S(1)} fusion(bf16[512,4096,1]{1,0,2:T(8,128)(2,1)} %reshape.324, bf16[8,128,4096]{2,1,0:T(8,128)(2,1)} %bitcast.146), kind=kOutput, calls=%fused_computation.84 | convolution fusion | flops 4294967296 | bytes 14680064 | tf_op jit(solution)/shard_map/dot_general | solution.py:89
  100.1 4.2 fusion.52
  104.7 4.1 fusion.44
  110.7 3.8 fusion.40
  114.5 7.2 %all-gather.7.cloned.1.call-done = bf16[64,2,64,256]{3,2,1,0:T(8,128)(2,1)} async-done(((bf16[8,2,64,256]{3,2,1,0:T(8,128)(2,1)}), bf16[64,2,64,256]{3,2,1,0:T(8,128)(2,1)}) %all-gather.7.cloned.1.call-update) | async-done | bytes 4194320 | tf_op jit(solution)/shard_map/all_gather | solution.py:111
  121.7 4.9 gather_fusion.3
  126.6 5.4 pad_maximum_fusion
  132.0 469.8 %while.10 = (s32[]{:T(128)}, bf16[16,8,4,2,4,128]{5,4,3,2,1,0:T(4,128)(2,1)}, s32[16,8,8]{2,1,0:T(8,128)S(1)}, bf16[96,2,64,256]{3,2,1,0:T(8,128)(2,1)}, s32[16,...) while((s32[]{:T(128)}, ...), condition=%wide.region_6.7_spmd, body=%wide.region_1.6_spmd.sunk | while | flops 69155288 | bytes 32177772 | solution.py:128
  132.1 5.6 gather_fusion.1
  137.7 4.0 slice_bitcast_fusion.4
  141.8 4.0 squeeze.40
  161.5 5.6 gather_fusion.1
  167.1 4.0 slice_bitcast_fusion.4
  171.1 4.0 squeeze.40
  190.8 5.6 gather_fusion.1
  196.5 4.0 slice_bitcast_fusion.4
  200.5 4.0 squeeze.40
  220.2 5.6 gather_fusion.1
  225.8 4.0 slice_bitcast_fusion.4
  229.9 4.0 squeeze.40
  249.6 5.6 gather_fusion.1
  255.2 4.0 slice_bitcast_fusion.4
  259.2 4.0 squeeze.40
  278.9 5.6 gather_fusion.1
  284.6 4.0 slice_bitcast_fusion.4
  288.6 4.0 squeeze.40
  308.3 5.6 gather_fusion.1
  313.9 4.0 slice_bitcast_fusion.4
  318.0 4.0 squeeze.40
  337.7 5.6 gather_fusion.1
  343.3 4.0 slice_bitcast_fusion.4
  347.3 4.0 squeeze.40
  367.0 5.6 gather_fusion.1
  372.7 4.0 slice_bitcast_fusion.4
  376.7 4.0 squeeze.40
  396.4 5.6 gather_fusion.1
  402.0 4.0 slice_bitcast_fusion.4
  406.0 4.0 squeeze.40
  425.8 5.6 gather_fusion.1
  431.4 4.0 slice_bitcast_fusion.4
  435.4 4.0 squeeze.40
  455.1 5.6 gather_fusion.1
  460.7 4.0 slice_bitcast_fusion.4
  464.8 4.0 squeeze.40
  484.5 5.6 gather_fusion.1
  490.1 4.0 slice_bitcast_fusion.4
  494.1 4.0 squeeze.40
  513.9 5.6 gather_fusion.1
  519.5 4.0 slice_bitcast_fusion.4
  523.5 4.0 squeeze.40
  543.2 5.6 gather_fusion.1
  548.8 4.0 slice_bitcast_fusion.4
  552.9 4.0 squeeze.40
  572.6 5.6 gather_fusion.1
  578.2 4.0 slice_bitcast_fusion.4
  582.2 4.0 squeeze.40
  603.6 9.4 %fusion.39 = bf16[4096,512]{0,1:T(8,128)(2,1)} fusion(bf16[512,1024]{1,0:T(8,128)(2,1)S(1)} %reshape.260, bf16[1024,4096]{1,0:T(8,128)(2,1)} %param.17), kind=kOutput, calls=%fused_computation.57 | convolution fusion | flops 4297064448 | bytes 13631488 | tf_op jit(solution)/shard_map/dot_general | solution.py:135
  613.1 42.9 %reduce-scatter.2.cloned.1.call-done = bf16[1024,512]{0,1:T(8,128)(2,1)} async-done(((bf16[4096,512]{0,1:T(8,128)(2,1)}), bf16[1024,512]{0,1:T(8,128)(2,1)}) %reduce-scatter.2.cloned.1.call-update) | async-done | bytes 1048592 | tf_op jit(solution)/shard_map/reduce_scatter | solution.py:134
  (514 shorter events, 273.9 us)
Async XLA Ops:
  6.5 56.4 %all-gather.5.cloned.1.call-start = ((), (), s32[]{:S(2)}) async-start(), calls=%async_computation.1 | async-start | bytes 5242880 | tf_op jit(solution)/shard_map/all_gather | solution.py:81
  7.3 114.4 %all-gather.7.cloned.1.call-start = ((), (), s32[]{:S(2)}) async-start(), calls=%async_computation.3 | async-start | bytes 4718592 | tf_op jit(solution)/shard_map/all_gather | solution.py:111
  11.0 645.0 %reduce-scatter.2.cloned.1.call-start = ((), (), s32[]{:S(2)}) async-start(), calls=%async_computation.2 | async-start | bytes 5242880 | tf_op jit(solution)/shard_map/reduce_scatter | solution.py:134
  11.1 11.8 %copy-start.5 = (s32[128]{0:T(128)S(1)}, s32[128]{0:T(128)}, u32[]{:S(2)}) copy-start(s32[128]{0:T(128)} %param.23) | copy-start | bytes 1540
  23.1 4.7 copy-start.4
  23.1 39.2 %copy-start.3 = (s32[128,8]{0,1:T(8,128)S(1)}, s32[128,8]{0,1:T(8,128)}, u32[]{:S(2)}) copy-start(s32[128,8]{0,1:T(8,128)} %param.22) | copy-start | bytes 12292
  24.9 42.7 %copy-start.2 = (f32[4096]{0:T(1024)S(1)}, f32[4096]{0:T(1024)}, u32[]{:S(2)}) copy-start(f32[4096]{0:T(1024)} %param.14) | copy-start | bytes 49156
  63.0 4.6 copy-start
  114.5 12.1 %copy-start.1 = (bf16[32,2,64,256]{3,2,1,0:T(8,128)(2,1)S(1)}, bf16[32,2,64,256]{3,2,1,0:T(8,128)(2,1)}, u32[]{:S(2)}) copy-start(bf16[32,2,64,256]{3,2,1,0:T(8,128)(2,1)} %param.18) | copy-start | bytes 6291460
  154.7 2.2 copy-start.6
  184.1 2.2 copy-start.6
  213.4 2.2 copy-start.6
  242.8 2.2 copy-start.6
  272.2 2.2 copy-start.6
  301.5 2.2 copy-start.6
  330.9 2.2 copy-start.6
  360.3 2.2 copy-start.6
  389.6 2.2 copy-start.6
  419.0 2.2 copy-start.6
  448.4 2.2 copy-start.6
  477.7 2.2 copy-start.6
  507.1 2.2 copy-start.6
  536.5 2.2 copy-start.6
  565.8 2.2 copy-start.6
  595.2 2.2 copy-start.6
Sparse Core Ops, SparseCore 0:
  8.9 37.1 all-gather.4
  48.3 73.3 all-gather.6
  613.2 42.7 reduce-scatter.1
where the time goes:
time: 670 us; the launch traced here: 665 us
  local copies, waits for them, and re-layouts  341 us (51%)
  matrix products  186 us (28%)
  waiting for transfers between devices  50.9 us (8%)
  other arithmetic  40.8 us (6%)
  blocking collectives  32.2 us (5%)
  between operations  13.3 us (2%)
    gather x16, local copies, waits for them, and re-layouts, one_block(): pool_codes[table]  89.9 us
    while x80, local copies, waits for them, and re-layouts  68.7 us
    squeeze x16, local copies, waits for them, and re-layouts, attend_block(): keys = codes[:, :, 0].reshape(blocks, slots, page, heads_here, HD)  64.4 us
    dot_general x16, matrix products, attend_block(): jnp.einsum('bthgmp,bmphd->bthgd', context_w, values, preferred_element_ty...  60.1 us
    dot_general x16, matrix products, attend_block(): jnp.einsum('bthgd,bmphd->bthgmp', query, keys, preferred_element_type=jnp...  59.1 us
    reduce_scatter x1, waiting for transfers between devices, per_device(): lax.psum_scatter(lax.dot_general(w_out, attended, (((0,), (1,)), ((), ())...  42.9 us
    squeeze x16, local copies, waits for them, and re-layouts, attend_block(): values = codes[:, :, 1].reshape(blocks, slots, page, heads_here, HD)  33.5 us
    all_gather x1, blocking collectives, per_device(): lax.all_gather(kv_scales[fork_export], 'branch', axis=0, tiled=True)  32.2 us
  transfers between devices with their start and end apart: 3, of which 2 were waited for; matrix products, arithmetic and copies ran while one was open for 11% of the time, Pallas kernels for 0%

commit v1 on v0

v1 whole, which is shorter than its diff:
```python
import functools
import math

import jax
import jax.numpy as jnp
from jax import lax
from jax.experimental import pallas as pl
from jax.experimental.pallas import tpu as pltpu
from jax.sharding import PartitionSpec as P

HEADS = 32
KVH = 8
HD = 128
STEPS = 4
GROUP = HEADS // KVH
NT = (((1,), (1,)), ((), ()))


def project_kernel(hid_ref, gain_ref, cos_ref, sin_ref, wq_ref, wkv_ref, q_ref, kn_ref, vn_ref,
                   weights, kv_weights, normed, tmp, q_rows, sems):
    parts, rows, width = hid_ref.shape
    branches = rows // STEPS
    q_tiles = wq_ref.shape[1] // 256
    copies = []
    for c in range(q_tiles):
        copies.append(pltpu.make_async_copy(wq_ref.at[:, pl.ds(c * 256, 256)], weights.at[c], sems.at[c]))
    for c in range(2):
        copies.append(pltpu.make_async_copy(wkv_ref.at[c], kv_weights.at[c], sems.at[q_tiles + c]))
    for copy in copies:
        copy.start()

    def norm_rows(r, _):
        at = pl.ds(pl.multiple_of(r * 64, 64), 64)
        power = jnp.zeros((64, 1), jnp.float32)
        for k in range(parts):
            v = hid_ref[k, at, :].astype(jnp.float32)
            power += jnp.sum(v * v, axis=-1, keepdims=True)
        inv = lax.rsqrt(power / (parts * width) + 1e-05)
        for k in range(parts):
            v = hid_ref[k, at, :].astype(jnp.float32)
            normed[at, k * width : (k + 1) * width] = (v * inv * gain_ref[k : k + 1, :]).astype(jnp.bfloat16)
        return 0

    lax.fori_loop(0, rows // 64, norm_rows, 0)

    def rope(v):
        return v * cos_ref[...] + pltpu.roll(v, HD // 2, 1) * sin_ref[...]

    for c in range(q_tiles + 2):
        copies[c].wait()
        tile = weights[c] if c < q_tiles else kv_weights[c - q_tiles]
        acc = jnp.dot(normed[...], tile, preferred_element_type=jnp.float32)
        if c < q_tiles:
            for i in range(2):
                tmp[...] = rope(acc[:, i * HD : (i + 1) * HD]) * HD ** (-0.5)
                head = c * 2 + i
                for t in range(STEPS):
                    q_rows[pl.ds(head * STEPS + t, branches, stride=q_tiles * 2 * STEPS), :] = tmp[
                        pl.ds(t, branches, stride=STEPS), :
                    ]
        elif c == q_tiles:
            for i in range(kv_weights.shape[2] // HD):
                kn_ref[:, i * HD : (i + 1) * HD] = rope(acc[:, i * HD : (i + 1) * HD]).astype(jnp.bfloat16)
        else:
            vn_ref[...] = acc.astype(jnp.bfloat16)
    q_ref[...] = q_rows[...].astype(jnp.bfloat16)


def attend_kernel(table_ref, lens_ref, q_ref, kn_ref, vn_ref, scale_ref, far_ref, own_ref, wo_ref,
                  out_ref, pool, scales, att_rows, tmp, att, sems):
    groups, far_rows = far_ref.shape[:2]
    own = own_ref.shape[0]
    per = (pool.shape[0] - own) // groups
    page = pool.shape[2]
    branches = lens_ref.shape[0]
    slots = table_ref.shape[0] // branches
    span = slots * page
    copies = [pltpu.make_async_copy(own_ref, pool.at[pl.ds(groups * per, own)], sems.at[groups])]
    for g in range(groups):
        copies.append(pltpu.make_async_copy(far_ref.at[g], pool.at[pl.ds(g * per, per)], sems.at[g]))
    for copy in copies:
        copy.start()
    spread = (
        lax.broadcasted_iota(jnp.int32, (slots, span), 1) // page
        == lax.broadcasted_iota(jnp.int32, (slots, span), 0)
    ).astype(jnp.bfloat16)
    scales[...] = jnp.dot(scale_ref[...], spread, preferred_element_type=jnp.float32)
    for copy in copies:
        copy.wait()

    kv_heads = kn_ref.shape[1] // HD
    deep = GROUP * STEPS
    each = deep * kv_heads
    row = lax.broadcasted_iota(jnp.int32, (8 * each, 1), 0)
    kv_head = (row % each) // deep
    col = lax.broadcasted_iota(jnp.int32, (8 * each, 32), 1)
    seen = ((col // STEPS) == (row // each)) & ((col % STEPS) <= (row % STEPS))
    token = lax.broadcasted_iota(jnp.int32, (1, span), 1)

    def block(b, _):
        at = pl.ds(pl.multiple_of(b * 8 * each, 8 * each), 8 * each)
        q = q_ref[at, :]
        zero = jnp.zeros_like(q)
        wide = jnp.concatenate([jnp.where(kv_head == h, q, zero) for h in range(kv_heads)], axis=1)
        new = pl.ds(pl.multiple_of(b * 32, 32), 32)
        fresh = lax.dot_general(wide, kn_ref[new, :], NT, preferred_element_type=jnp.float32)
        fresh = jnp.where(seen, fresh, -1e30)
        fresh_top = jnp.max(fresh, axis=1, keepdims=True)
        outs, tops, sums = [], [], []
        for i in range(8):
            n = b * 8 + i
            ids = [table_ref[n * slots + m] for m in range(slots)]
            keys = jnp.concatenate([pool[x, 0] for x in ids], axis=0)
            s = lax.dot_general(wide[i * each : (i + 1) * each], keys, NT, preferred_element_type=jnp.float32)
            sc = scales[pl.ds(pl.multiple_of(n * 8, 8), 8), :]
            ks, vs = (
                jnp.concatenate(
                    [
                        jnp.broadcast_to(sc[j * kv_heads + h : j * kv_heads + h + 1], (deep, span))
                        for h in range(kv_heads)
                    ],
                    axis=0,
                )
                for j in range(2)
            )
            s = jnp.where(token < lens_ref[n], s * ks, -1e30)
            top = jnp.maximum(jnp.max(s, axis=1, keepdims=True), fresh_top[i * each : (i + 1) * each])
            e = jnp.exp(s - top)
            tops.append(top)
            sums.append(jnp.sum(e, axis=1, keepdims=True))
            values = jnp.concatenate([pool[x, 1] for x in ids], axis=0)
            outs.append(
                jnp.dot((e * vs).astype(jnp.bfloat16), values, preferred_element_type=jnp.float32)
            )
        fresh_e = jnp.exp(fresh - jnp.concatenate(tops, axis=0))
        total = jnp.concatenate(sums, axis=0) + jnp.sum(fresh_e, axis=1, keepdims=True)
        out = jnp.concatenate(outs, axis=0) + jnp.dot(
            fresh_e.astype(jnp.bfloat16), vn_ref[new, :], preferred_element_type=jnp.float32
        )
        picked = out[:, :HD]
        for h in range(1, kv_heads):
            picked = jnp.where(kv_head == h, out[:, h * HD : (h + 1) * HD], picked)
        att_rows[at, :] = picked / total
        return 0

    lax.fori_loop(0, branches // 8, block, 0)

    heads = att.shape[1] // HD
    for head in range(heads):
        for t in range(STEPS):
            tmp[pl.ds(t, branches, stride=STEPS), :] = att_rows[
                pl.ds(head * STEPS + t, branches, stride=heads * STEPS), :
            ]
        att[:, head * HD : (head + 1) * HD] = tmp[...].astype(jnp.bfloat16)

    parts = out_ref.shape[0]
    width = out_ref.shape[2]

    def project(j, _):
        for k in range(parts):
            cols = pl.ds(pl.multiple_of(k * width + j * 256, 256), 256)
            out_ref[k, :, pl.ds(pl.multiple_of(j * 256, 256), 256)] = jnp.dot(
                att[...], wo_ref[:, cols], preferred_element_type=jnp.float32
            ).astype(jnp.bfloat16)
        return 0

    lax.fori_loop(0, width // 256, project, 0)


def per_device(hidden, gain, w_query, w_keyval, w_out, kv_codes, kv_scales, fork_export, fork_pull,
               page_table, lengths):
    branches, steps, width = hidden.shape
    rows = branches * steps
    parts = lax.axis_size("tensor")
    own, _, page, kv_cols = kv_codes.shape
    per = fork_export.shape[0]
    heads_here = kv_cols // HD
    full = lax.all_gather(hidden.reshape(rows, width), "tensor", axis=0, tiled=False)

    positions = (lengths[:, None] + jnp.arange(steps, dtype=jnp.int32)[None, :]).reshape(-1)
    half = HD // 2
    freq = jnp.exp(-(2.0 * jnp.arange(half).astype(jnp.float32) / HD) * math.log(500000.0))
    angle = positions.astype(jnp.float32)[:, None] * freq[None, :]
    cosine, sine = jnp.cos(angle), jnp.sin(angle)
    cosine = jnp.concatenate([cosine, cosine], axis=1)
    sine = jnp.concatenate([-sine, sine], axis=1)

    myself = lax.axis_index("branch")
    my_row = lax.dynamic_index_in_dim(fork_pull, myself, 0, keepdims=False)
    offered = kv_codes[fork_export].reshape(per * 2 * page, kv_cols)
    tail = jnp.zeros((16, kv_cols), jnp.bfloat16)
    tail = tail.at[0, : per * 2 * heads_here].set(kv_scales[fork_export].reshape(-1))
    every = lax.all_gather(jnp.concatenate([offered, tail], axis=0), "branch", axis=0, tiled=False)
    groups = every.shape[0]
    far = every[:, : per * 2 * page].reshape(groups, per, 2, page, kv_cols)
    far_scales = every[:, per * 2 * page, : per * 2 * heads_here].reshape(groups * per, 2 * heads_here)

    pool_ids = jnp.concatenate([my_row, jnp.arange(own, dtype=jnp.int32) + groups * per])
    pool_scales = jnp.concatenate([far_scales, kv_scales.reshape(own, 2 * heads_here)], axis=0)
    table = pool_ids[page_table]
    slots = table.shape[1]
    scale = jnp.pad(jnp.transpose(pool_scales[table], (0, 2, 1)), ((0, 0), (0, 8 - 2 * heads_here), (0, 0)))
    scale = scale.reshape(branches * 8, slots)

    heads = w_query.shape[1] // HD
    q_tiles = w_query.shape[1] // 256
    vmem = pl.BlockSpec(memory_space=pltpu.VMEM)
    anywhere = pl.BlockSpec(memory_space=pl.ANY)
    smem = pl.BlockSpec(memory_space=pltpu.SMEM)
    query, key_new, value_new = pl.pallas_call(
        project_kernel,
        out_shape=(
            jax.ShapeDtypeStruct((branches * heads * steps, HD), jnp.bfloat16),
            jax.ShapeDtypeStruct((rows, kv_cols), jnp.bfloat16),
            jax.ShapeDtypeStruct((rows, kv_cols), jnp.bfloat16),
        ),
        in_specs=[vmem, vmem, vmem, vmem, anywhere, anywhere],
        out_specs=(vmem, vmem, vmem),
        scratch_shapes=[
            pltpu.VMEM((q_tiles, parts * width, 256), jnp.bfloat16),
            pltpu.VMEM((2, parts * width, kv_cols), jnp.bfloat16),
            pltpu.VMEM((rows, parts * width), jnp.bfloat16),
            pltpu.VMEM((rows, HD), jnp.float32),
            pltpu.VMEM((branches * heads * steps, HD), jnp.float32),
            pltpu.SemaphoreType.DMA((q_tiles + 2,)),
        ],
        compiler_params=pltpu.CompilerParams(vmem_limit_bytes=48 * 2**20),
    )(full, gain.reshape(parts, width), cosine, sine, w_query, w_keyval)

    partial = pl.pallas_call(
        attend_kernel,
        out_shape=jax.ShapeDtypeStruct((parts, rows, width), jnp.bfloat16),
        in_specs=[smem, smem, vmem, vmem, vmem, vmem, anywhere, anywhere, vmem],
        out_specs=vmem,
        scratch_shapes=[
            pltpu.VMEM((groups * per + own, 2, page, kv_cols), jnp.bfloat16),
            pltpu.VMEM((branches * 8, slots * page), jnp.float32),
            pltpu.VMEM((branches * heads * steps, HD), jnp.float32),
            pltpu.VMEM((rows, HD), jnp.float32),
            pltpu.VMEM((rows, heads * HD), jnp.bfloat16),
            pltpu.SemaphoreType.DMA((groups + 1,)),
        ],
        compiler_params=pltpu.CompilerParams(vmem_limit_bytes=48 * 2**20),
    )(table.reshape(-1), lengths, query, key_new, value_new, scale, far, kv_codes, w_out)
    mixed = lax.psum_scatter(partial, "tensor", scatter_dimension=0, tiled=False)
    return mixed.reshape(branches, steps, width)


def solution(mesh):
    return jax.shard_map(
        per_device,
        mesh=mesh,
        in_specs=(
            P("branch", None, "tensor"),
            P(),
            P(None, "tensor"),
            P(None, None, "tensor"),
            P("tensor", None),
            P("branch", None, None, "tensor"),
            P("branch", None, "tensor"),
            P("branch"),
            P(),
            P("branch", None),
            P("branch"),
        ),
        out_specs=P("branch", None, "tensor"),
        check_vma=False,
    )
```

time: 670 us -> 250 us (0.37)
  local copies, waits for them, and re-layouts: 341 us -> 30 us
  matrix products: 186 us -> 0 us
  Pallas kernels: 0 us -> 81.2 us
  waiting for transfers between devices: 50.9 us -> 122 us
  other arithmetic: 40.8 us -> 2.95 us
  blocking collectives: 32.2 us -> 0 us
    dot_general x68 -> x0, matrix products: 186 us -> none  [the longest x16 60.1 us: attend_block(): jnp.einsum('bthgmp,bmphd->bthgd', context_w, values, preferred_element_ty...]
    squeeze x32 -> x1, local copies, waits for them, and re-layouts: 97.9 us -> 0.01 us  [per_device(): my_row = lax.dynamic_index_in_dim(fork_pull, myself, 0, keepdims=False)]
    gather x37 -> x6, local copies, waits for them, and re-layouts: 109 us -> 16.1 us  [the longest x2 6.73 us: per_device(): pool_scales[table]]
    pallas_call x0 -> x2, Pallas kernels: none -> 81.2 us  [the longest x1 61.2 us: per_device(): pl.pallas_call(attend_kernel, out_shape=jax.ShapeDtypeStruct((parts, rows...]
    all_gather x2, waiting for transfers between devices: 7.2 us -> 79.1 us  [the longest x1 55.7 us: per_device(): lax.all_gather(jnp.concatenate([offered, tail], axis=0), 'branch', axis=0...]
    while x81 -> x0, local copies, waits for them, and re-layouts: 68.8 us -> none
    all_gather x1 -> x0, blocking collectives: 32.2 us -> none  [per_device(): lax.all_gather(kv_scales[fork_export], 'branch', axis=0, tiled=True)]
    reduce_sum x33 -> x0, other arithmetic: 18.7 us -> none  [the longest x32 14.1 us: attend_block(): total = jnp.sum(context_exp, axis=(4, 5)) + jnp.sum(fresh_exp, axis=4)]
  transfers between devices with their start and end apart: 3 -> 3, of which waited for: 2 -> 3; matrix products, arithmetic and copies ran while one was open for 11% -> 5% of each run, Pallas kernels for 0% -> 8%
where the time goes in v1:
time: 250 us
  waiting for transfers between devices  122 us (49%)
  Pallas kernels  81.2 us (32%)
  local copies, waits for them, and re-layouts  30 us (12%)
  between operations  13.3 us (5%)
  other arithmetic  2.95 us (1%)
    pallas_call x1, Pallas kernels, per_device(): pl.pallas_call(attend_kernel, out_shape=jax.ShapeDtypeStruct((parts, rows...  61.2 us
    all_gather x1, waiting for transfers between devices, per_device(): lax.all_gather(jnp.concatenate([offered, tail], axis=0), 'branch', axis=0...  55.7 us
    reduce_scatter x1, waiting for transfers between devices, per_device(): lax.psum_scatter(partial, 'tensor', scatter_dimension=0, tiled=False)  42.9 us
    all_gather x1, waiting for transfers between devices, per_device(): lax.all_gather(hidden.reshape(rows, width), 'tensor', axis=0, tiled=False)  23.4 us
    pallas_call x1, Pallas kernels, per_device(): pl.pallas_call(project_kernel, out_shape=(jax.ShapeDtypeStruct((branches...  20 us
    gather x2, local copies, waits for them, and re-layouts, per_device(): pool_scales[table]  6.73 us
    gather x2, local copies, waits for them, and re-layouts, per_device(): table = pool_ids[page_table]  6.64 us
  transfers between devices with their start and end apart: 3, of which 3 were waited for; matrix products, arithmetic and copies ran while one was open for 5% of the time, Pallas kernels for 8%

profile of v1, /device:TPU:0, one launch (start us, length us, event | category | flops | bytes accessed | tf_op | source)
XLA Modules:
  0.0 249.6 jit_solution(11517966286584605571)
XLA Ops:
  6.5 0.0 copy-start
  6.5 0.0 copy-start.4
  6.5 0.0 copy-start.5
  6.5 0.0 copy-start.7
  6.5 0.0 all-gather.4.cloned.1.call-start
  6.6 2.1 all_gather_reshape.3
  8.7 0.0 all-gather.4.cloned.1.call-update
  8.8 0.0 all-gather.6.cloned.1.call-start
  8.8 0.8 copy.30
  9.6 0.7 compare_select_fusion.2
  10.3 2.2 gather_fusion.1
  12.4 0.6 gather_fusion.2
  13.0 0.1 reshape.91
  13.1 0.9 fusion.1
  14.0 0.0 all-gather.6.cloned.1.call-update
  14.0 0.0 reduce-scatter.2.cloned.1.call-start
  14.1 0.0 copy-done.4
  14.1 0.1 add_convert_fusion
  14.2 0.1 convert_element_type.20
  14.3 0.0 copy-done.5
  14.3 0.0 copy-done.7
  14.3 0.1 copy.29
  14.4 0.1 reshape.97
  14.5 0.0 copy-done
  14.6 0.1 pad_add_fusion
  14.6 0.0 copy-start.6
  14.6 6.6 %gather_fusion = s32[1024]{0:T(1024)S(1)} fusion(s32[96]{0:T(128)S(1)} %pad_add_fusion, s32[1024]{0:T(1024)S(1)} %broadcast_clamp_fusion.1), kind=kCustom, calls=%fused_computation | custom fusion | bytes 12288 | tf_op jit(solution)/shard_map/gather | solution.py:200
  21.2 0.1 gather.17
  21.3 0.1 reshape.121
  21.4 0.0 copy-done.6
  21.4 0.1 copy.31
  21.5 1.0 fusion.2
  22.5 0.2 pad_maximum_fusion
  22.8 23.4 %all-gather.4.cloned.1.call-done.hid_ref = bf16[4,512,1024]{2,1,0:T(8,128)(2,1)} async-done(((bf16[1,512,1024]{2,1,0:T(8,128)(2,1)}), bf16[4,512,1024]{2,1,0:T(8,128)(2,1)}) %all-gather.4.cloned.1.call-update) | async-done | bytes 4194320 | tf_op jit(solution)/shard_map/all_gather | solution.py:178
  46.2 20.0 %shard_map.109 = (bf16[4096,128]{1,0:T(8,128)(2,1)S(1)}, bf16[512,256]{1,0:T(8,128)(2,1)S(1)}, bf16[512,256]{1,0:T(8,128)(2,1)S(1)}) custom-call(bf16[4,512,1024]{2,1,0:T(8,128)(2,1)} %all-gather.4.cloned.1.call-done.hid_ref, f32[4,1024]{1,0:T(4,128)S(1)} %reshape.89.gain_ref, f32[512,128]{1,0:T(8,128)S(1)} %get-tuple-element.26.cos_ref, ...), custom_call_target="tpu_custom_call" | custom-call | tf_op jit(solution)/shard_map/pallas_call | solution.py:210
  66.2 0.0 copy-start.2
  66.2 0.7 copy-done.2
  66.9 55.7 %all-gather.6.cloned.1.call-done = bf16[8320,256]{1,0:T(8,128)(2,1)} async-done(((bf16[1040,256]{1,0:T(8,128)(2,1)}), bf16[8320,256]{1,0:T(8,128)(2,1)}) %all-gather.6.cloned.1.call-update) | async-done | bytes 4259856 | tf_op jit(solution)/shard_map/all_gather | solution.py:193
  122.6 0.7 slice_reduce_fusion
  123.3 0.0 copy-start.1
  123.3 4.6 %slice.33 = bf16[8,1024,256]{2,1,0:T(8,128)(2,1)} slice(bf16[8,1040,256]{2,1,0:T(8,128)(2,1)} %bitcast.14), slice={[0:8], [0:1024], [0:256]} | slice | bytes 8388608 | tf_op jit(solution)/shard_map/slice | solution.py:195
  127.9 0.1 reshape_squeeze.3
  128.0 4.3 %gather_fusion.3 = bf16[1024,4]{1,0:T(8,128)(2,1)} fusion(bf16[96,4]{1,0:T(8,128)(2,1)S(1)} %pad_maximum_fusion.2, s32[1024]{0:T(1024)S(1)} %broadcast_clamp_fusion), kind=kCustom, calls=%fused_computation.3 | custom fusion | bytes 20480 | tf_op jit(solution)/shard_map/gather | solution.py:202
  132.3 2.4 copy.32
  134.7 1.0 pad_bitcast_fusion.scale_ref
  135.7 0.0 copy-done.1
  135.7 0.0 copy-start.3
  135.7 0.9 copy-done.3
  136.7 61.2 %shard_map.110 = bf16[4,512,1024]{2,1,0:T(8,128)(2,1)} custom-call(s32[1024]{0:T(1024)S(1)} %gather_fusion, s32[128]{0:T(128)S(1)} %copy-done.4, bf16[4096,128]{1,0:T(8,128)(2,1)S(1)} %get-tuple-element.20.q_ref, bf16[512,256]{1,0:T(8,128)(2,1)S(1)} %get-tuple-element.21.kn_ref, bf16[512,256]{1,0:T(8,128)(2,1)S(1)} %copy-done.3, ...), custom_call_target="tpu_custom_call" | custom-call | tf_op jit(solution)/shard_map/pallas_call | solution.py:230
  197.9 0.0 reduce-scatter.2.cloned.1.call-update
  197.9 42.9 %reduce-scatter.2.cloned.1.call-done = bf16[1,512,1024]{2,1,0:T(8,128)(2,1)} async-done(((bf16[4,512,1024]{2,1,0:T(8,128)(2,1)}), bf16[1,512,1024]{2,1,0:T(8,128)(2,1)}) %reduce-scatter.2.cloned.1.call-update) | async-done | bytes 1048592 | tf_op jit(solution)/shard_map/reduce_scatter | solution.py:245
  240.8 2.2 reshape_reduce_scatter.3
  (10 shorter events, 0.1 us)
Async XLA Ops:
  6.5 8.0 %copy-start = (s32[8,64]{1,0:T(8,128)S(1)}, s32[8,64]{1,0:T(8,128)}, u32[]{:S(2)}) copy-start(s32[8,64]{1,0:T(8,128)} %param.21) | copy-start | bytes 6148
  6.5 7.5 %copy-start.4 = (s32[128]{0:T(128)S(1)}, s32[128]{0:T(128)}, u32[]{:S(2)}) copy-start(s32[128]{0:T(128)} %lens_ref.1) | copy-start | bytes 1540
  6.5 7.7 %copy-start.5 = (f32[4096]{0:T(1024)S(1)}, f32[4096]{0:T(1024)}, u32[]{:S(2)}) copy-start(f32[4096]{0:T(1024)} %param.14) | copy-start | bytes 49156
  6.5 7.8 %copy-start.7 = (s32[128,8]{0,1:T(8,128)S(1)}, s32[128,8]{0,1:T(8,128)}, u32[]{:S(2)}) copy-start(s32[128,8]{0,1:T(8,128)} %param.22) | copy-start | bytes 12292
  6.5 39.6 %all-gather.4.cloned.1.call-start = ((), (), s32[]{:S(2)}) async-start(), calls=%async_computation.1 | async-start | bytes 5242880 | tf_op jit(solution)/shard_map/all_gather | solution.py:178
  8.8 113.8 %all-gather.6.cloned.1.call-start = ((), (), s32[]{:S(2)}) async-start(), calls=%async_computation.3 | async-start | bytes 4792320 | tf_op jit(solution)/shard_map/all_gather | solution.py:193
  14.0 226.8 %reduce-scatter.2.cloned.1.call-start = ((), (), s32[]{:S(2)}) async-start(), calls=%async_computation.2 | async-start | bytes 5242880 | tf_op jit(solution)/shard_map/reduce_scatter | solution.py:245
  14.6 6.8 %copy-start.6 = (bf16[32,2,2]{0,2,1:T(2,128)(2,1)S(1)}, bf16[32,2,2]{0,2,1:T(2,128)(2,1)}, u32[]{:S(2)}) copy-start(bf16[32,2,2]{0,2,1:T(2,128)(2,1)} %param.19) | copy-start | bytes 772
  66.2 0.7 copy-start.2
  123.3 12.4 %copy-start.1 = (bf16[32,2,64,256]{3,2,1,0:T(8,128)(2,1)S(1)}, bf16[32,2,64,256]{3,2,1,0:T(8,128)(2,1)}, u32[]{:S(2)}) copy-start(bf16[32,2,64,256]{3,2,1,0:T(8,128)(2,1)} %own_ref.1) | copy-start | bytes 6291460
  135.7 1.0 copy-start.3
Sparse Core Ops, SparseCore 0:
  8.9 37.1 all-gather.3
  48.3 74.1 all-gather.5
  198.0 42.7 reduce-scatter.1

commit v2 on v1

--- a/solution.py
+++ b/solution.py
@@ -66,25 +66,101 @@
     q_ref[...] = q_rows[...].astype(jnp.bfloat16)
 
 
-def attend_kernel(table_ref, lens_ref, q_ref, kn_ref, vn_ref, scale_ref, far_ref, own_ref, wo_ref,
+def offer_kernel(export_ref, codes_ref, tail_ref, out_ref, sems):
+    per = export_ref.shape[0]
+    rows = (out_ref.shape[0] - tail_ref.shape[0]) // per
+    copies = [
+        pltpu.make_async_copy(
+            codes_ref.at[pl.ds(pl.multiple_of(export_ref[j] * rows, rows), rows)],
+            out_ref.at[pl.ds(j * rows, rows)],
+            sems.at[j],
+        )
+        for j in range(per)
+    ]
+    copies.append(
+        pltpu.make_async_copy(tail_ref, out_ref.at[pl.ds(per * rows, tail_ref.shape[0])], sems.at[per])
+    )
+    for copy in copies:
+        copy.start()
+    for copy in copies:
+        copy.wait()
+
+
+def exchange_kernel(far, near, mine_ref, every_ref, local_sem, send_far, recv_far, send_near, recv_near):
+    me = lax.axis_index("branch")
+    line, place = me // near, me % near
+
+    def far_peer(k):
+        return ((line + k) % far) * near + place
+
+    def near_peer(j):
+        return line * near + (place + j) % near
+
+    def push(src, block, peer, send_sem, recv_sem):
+        copy = pltpu.make_async_remote_copy(
+            src_ref=src,
+            dst_ref=every_ref.at[block],
+            send_sem=send_sem,
+            recv_sem=recv_sem,
+            device_id={"branch": peer},
+            device_id_type=pl.DeviceIdType.MESH,
+        )
+        copy.start()
+        return copy
+
+    barrier = pltpu.get_barrier_semaphore()
+    peers = [far_peer(k) for k in range(1, far)] + [near_peer(j) for j in range(1, near)]
+    for peer in peers:
+        pl.semaphore_signal(
+            barrier, inc=1, device_id={"branch": peer}, device_id_type=pl.DeviceIdType.MESH
+        )
+    pl.semaphore_wait(barrier, len(peers))
+
+    order = sorted(range(1, far), key=lambda k: min(k, far - k))
+    sent_far = {k: push(mine_ref, me, far_peer(k), send_far.at[k - 1], recv_far.at[k - 1]) for k in order}
+    sent_near = [
+        push(mine_ref, me, near_peer(j), send_near.at[0, j - 1], recv_near.at[0, j - 1])
+        for j in range(1, near)
+    ]
+    own = pltpu.make_async_copy(mine_ref, every_ref.at[me], local_sem)
+    own.start()
+    for k in order:
+        sent_far[k].wait_recv()
+        block = ((line + far - k) % far) * near + place
+        for j in range(1, near):
+            sent_near.append(
+                push(
+                    every_ref.at[block], block, near_peer(j), send_near.at[k, j - 1], recv_near.at[k, j - 1]
+                )
+            )
+    for copy in sent_near:
+        copy.wait_recv()
+    for k in order:
+        sent_far[k].wait_send()
+    for copy in sent_near:
+        copy.wait_send()
+    own.wait()
+
+
+def attend_kernel(begin, branches, table_ref, lens_ref, q_ref, kn_ref, vn_ref, scale_ref, far_ref, own_ref, wo_ref,
                   out_ref, pool, scales, att_rows, tmp, att, sems):
-    groups, far_rows = far_ref.shape[:2]
-    own = own_ref.shape[0]
-    per = (pool.shape[0] - own) // groups
-    page = pool.shape[2]
-    branches = lens_ref.shape[0]
-    slots = table_ref.shape[0] // branches
+    groups = far_ref.shape[0]
+    slots = table_ref.shape[0] // lens_ref.shape[0]
+    page = scales.shape[1] // slots
+    per = (pool.shape[0] - own_ref.shape[0]) // (groups * 2 * page)
     span = slots * page
-    copies = [pltpu.make_async_copy(own_ref, pool.at[pl.ds(groups * per, own)], sems.at[groups])]
+    copies = [
+        pltpu.make_async_copy(own_ref, pool.at[pl.ds(groups * per * 2 * page, own_ref.shape[0])], sems.at[groups])
+    ]
     for g in range(groups):
-        copies.append(pltpu.make_async_copy(far_ref.at[g], pool.at[pl.ds(g * per, per)], sems.at[g]))
+        copies.append(pltpu.make_async_copy(far_ref.at[g, pl.ds(0, per * 2 * page)], pool.at[pl.ds(g * per * 2 * page, per * 2 * page)], sems.at[g]))
     for copy in copies:
         copy.start()
     spread = (
         lax.broadcasted_iota(jnp.int32, (slots, span), 1) // page
         == lax.broadcasted_iota(jnp.int32, (slots, span), 0)
     ).astype(jnp.bfloat16)
-    scales[...] = jnp.dot(scale_ref[...], spread, preferred_element_type=jnp.float32)
+    scales[...] = jnp.dot(scale_ref[pl.ds(begin * 8, branches * 8), :], spread, preferred_element_type=jnp.float32)
     for copy in copies:
         copy.wait()
 
@@ -99,20 +175,20 @@
 
     def block(b, _):
         at = pl.ds(pl.multiple_of(b * 8 * each, 8 * each), 8 * each)
-        q = q_ref[at, :]
+        q = q_ref[pl.ds(pl.multiple_of(begin * each + b * 8 * each, 8 * each), 8 * each), :]
         zero = jnp.zeros_like(q)
         wide = jnp.concatenate([jnp.where(kv_head == h, q, zero) for h in range(kv_heads)], axis=1)
-        new = pl.ds(pl.multiple_of(b * 32, 32), 32)
+        new = pl.ds(pl.multiple_of(begin * STEPS + b * 32, 32), 32)
         fresh = lax.dot_general(wide, kn_ref[new, :], NT, preferred_element_type=jnp.float32)
         fresh = jnp.where(seen, fresh, -1e30)
         fresh_top = jnp.max(fresh, axis=1, keepdims=True)
         outs, tops, sums = [], [], []
         for i in range(8):
-            n = b * 8 + i
+            n = begin + b * 8 + i
             ids = [table_ref[n * slots + m] for m in range(slots)]
-            keys = jnp.concatenate([pool[x, 0] for x in ids], axis=0)
+            keys = jnp.concatenate([pool[pl.ds(pl.multiple_of(x * 2 * page, 2 * page), page), :] for x in ids], axis=0)
             s = lax.dot_general(wide[i * each : (i + 1) * each], keys, NT, preferred_element_type=jnp.float32)
-            sc = scales[pl.ds(pl.multiple_of(n * 8, 8), 8), :]
+            sc = scales[pl.ds(pl.multiple_of((n - begin) * 8, 8), 8), :]
             ks, vs = (
                 jnp.concatenate(
                     [
@@ -128,7 +204,7 @@
             e = jnp.exp(s - top)
             tops.append(top)
             sums.append(jnp.sum(e, axis=1, keepdims=True))
-            values = jnp.concatenate([pool[x, 1] for x in ids], axis=0)
+            values = jnp.concatenate([pool[pl.ds(pl.multiple_of(x * 2 * page + page, page), page), :] for x in ids], axis=0)
             outs.append(
                 jnp.dot((e * vs).astype(jnp.bfloat16), values, preferred_element_type=jnp.float32)
             )
@@ -187,26 +263,51 @@
 
     myself = lax.axis_index("branch")
     my_row = lax.dynamic_index_in_dim(fork_pull, myself, 0, keepdims=False)
-    offered = kv_codes[fork_export].reshape(per * 2 * page, kv_cols)
-    tail = jnp.zeros((16, kv_cols), jnp.bfloat16)
-    tail = tail.at[0, : per * 2 * heads_here].set(kv_scales[fork_export].reshape(-1))
-    every = lax.all_gather(jnp.concatenate([offered, tail], axis=0), "branch", axis=0, tiled=False)
-    groups = every.shape[0]
-    far = every[:, : per * 2 * page].reshape(groups, per, 2, page, kv_cols)
+    vmem = pl.BlockSpec(memory_space=pltpu.VMEM)
+    anywhere = pl.BlockSpec(memory_space=pl.ANY)
+    smem = pl.BlockSpec(memory_space=pltpu.SMEM)
+    groups = lax.axis_size("branch")
+    near = 2 ** (int(math.log2(groups)) // 2)
+    pages = kv_codes.reshape(own, 2 * page, kv_cols)
+    tail = jnp.pad(
+        kv_scales[fork_export].reshape(1, -1), ((0, 15), (0, kv_cols - per * 2 * heads_here))
+    )
+    offered = pl.pallas_call(
+        offer_kernel,
+        out_shape=jax.ShapeDtypeStruct((per * 2 * page + 16, kv_cols), jnp.bfloat16),
+        in_specs=[smem, anywhere, anywhere],
+        out_specs=anywhere,
+        scratch_shapes=[pltpu.SemaphoreType.DMA((per + 1,))],
+    )(fork_export, pages.reshape(own * 2 * page, kv_cols), tail)
+    far_count = groups // near
+    every = pl.pallas_call(
+        functools.partial(exchange_kernel, far_count, near),
+        out_shape=jax.ShapeDtypeStruct((groups,) + offered.shape, jnp.bfloat16),
+        in_specs=[anywhere],
+        out_specs=anywhere,
+        scratch_shapes=[
+            pltpu.SemaphoreType.DMA,
+            pltpu.SemaphoreType.DMA((far_count - 1,)),
+            pltpu.SemaphoreType.DMA((far_count - 1,)),
+            pltpu.SemaphoreType.DMA((far_count, near - 1)),
+            pltpu.SemaphoreType.DMA((far_count, near - 1)),
+        ],
+        compiler_params=pltpu.CompilerParams(collective_id=0, has_side_effects=True),
+        cost_estimate=pl.CostEstimate(flops=0, bytes_accessed=150 * 2**20, transcendentals=0),
+    )(offered)
     far_scales = every[:, per * 2 * page, : per * 2 * heads_here].reshape(groups * per, 2 * heads_here)
 
     pool_ids = jnp.concatenate([my_row, jnp.arange(own, dtype=jnp.int32) + groups * per])
     pool_scales = jnp.concatenate([far_scales, kv_scales.reshape(own, 2 * heads_here)], axis=0)
     table = pool_ids[page_table]
     slots = table.shape[1]
-    scale = jnp.pad(jnp.transpose(pool_scales[table], (0, 2, 1)), ((0, 0), (0, 8 - 2 * heads_here), (0, 0)))
+    chosen = (table[:, :, None] == jnp.arange(groups * per + own)).astype(jnp.bfloat16)
+    padded = jnp.pad(pool_scales, ((0, 0), (0, 8 - 2 * heads_here)))
+    scale = jnp.einsum("nmp,pj->njm", chosen, padded, preferred_element_type=jnp.float32).astype(jnp.bfloat16)
     scale = scale.reshape(branches * 8, slots)
 
     heads = w_query.shape[1] // HD
     q_tiles = w_query.shape[1] // 256
-    vmem = pl.BlockSpec(memory_space=pltpu.VMEM)
-    anywhere = pl.BlockSpec(memory_space=pl.ANY)
-    smem = pl.BlockSpec(memory_space=pltpu.SMEM)
     query, key_new, value_new = pl.pallas_call(
         project_kernel,
         out_shape=(
@@ -227,23 +328,30 @@
         compiler_params=pltpu.CompilerParams(vmem_limit_bytes=48 * 2**20),
     )(full, gain.reshape(parts, width), cosine, sine, w_query, w_keyval)
 
-    partial = pl.pallas_call(
-        attend_kernel,
-        out_shape=jax.ShapeDtypeStruct((parts, rows, width), jnp.bfloat16),
-        in_specs=[smem, smem, vmem, vmem, vmem, vmem, anywhere, anywhere, vmem],
-        out_specs=vmem,
-        scratch_shapes=[
-            pltpu.VMEM((groups * per + own, 2, page, kv_cols), jnp.bfloat16),
-            pltpu.VMEM((branches * 8, slots * page), jnp.float32),
-            pltpu.VMEM((branches * heads * steps, HD), jnp.float32),
-            pltpu.VMEM((rows, HD), jnp.float32),
-            pltpu.VMEM((rows, heads * HD), jnp.bfloat16),
-            pltpu.SemaphoreType.DMA((groups + 1,)),
-        ],
-        compiler_params=pltpu.CompilerParams(vmem_limit_bytes=48 * 2**20),
-    )(table.reshape(-1), lengths, query, key_new, value_new, scale, far, kv_codes, w_out)
-    mixed = lax.psum_scatter(partial, "tensor", scatter_dimension=0, tiled=False)
-    return mixed.reshape(branches, steps, width)
+    half_count = branches // 2
+    done = []
+    for part in range(2):
+        partial = pl.pallas_call(
+            functools.partial(attend_kernel, part * half_count, half_count),
+            out_shape=jax.ShapeDtypeStruct((parts, half_count * steps, width), jnp.bfloat16),
+            in_specs=[smem, smem, vmem, vmem, vmem, vmem, anywhere, anywhere, vmem],
+            out_specs=vmem,
+            scratch_shapes=[
+                pltpu.VMEM(((groups * per + own) * 2 * page, kv_cols), jnp.bfloat16),
+                pltpu.VMEM((half_count * 8, slots * page), jnp.float32),
+                pltpu.VMEM((half_count * heads * steps, HD), jnp.float32),
+                pltpu.VMEM((half_count * steps, HD), jnp.float32),
+                pltpu.VMEM((half_count * steps, heads * HD), jnp.bfloat16),
+                pltpu.SemaphoreType.DMA((groups + 1,)),
+            ],
+            compiler_params=pltpu.CompilerParams(vmem_limit_bytes=48 * 2**20),
+            cost_estimate=pl.CostEstimate(
+                flops=20 * 10**9, bytes_accessed=90 * 2**20, transcendentals=half_count * heads * steps * slots * page
+            ),
+        )(table.reshape(-1), lengths, query, key_new, value_new, scale, every,
+          pages.reshape(own * 2 * page, kv_cols), w_out)
+        done.append(lax.psum_scatter(partial, "tensor", scatter_dimension=0, tiled=False))
+    return jnp.concatenate(done, axis=0).reshape(branches, steps, width)
 
 
 def solution(mesh):

time: 250 us -> 236 us (0.944)
  waiting for transfers between devices: 122 us -> 29.3 us
  Pallas kernels: 81.2 us -> 170 us
  local copies, waits for them, and re-layouts: 30 us -> 18.5 us
    pallas_call x1 -> x4, Pallas kernels: 61.2 us -> 150 us  [the longest x1 66.2 us: per_device(): pl.pallas_call(functools.partial(exchange_kernel, far_count, near), out_s...]
    all_gather x1 -> x0, waiting for transfers between devices: 55.7 us -> none  [per_device(): lax.all_gather(jnp.concatenate([offered, tail], axis=0), 'branch', axis=0...]
    all_gather x1, waiting for transfers between devices: 23.4 us -> 0.02 us  [per_device(): lax.all_gather(hidden.reshape(rows, width), 'tensor', axis=0, tiled=False)]
    reduce_scatter x1 -> x2, waiting for transfers between devices: 42.9 us -> 29.3 us  [per_device(): lax.psum_scatter(partial, 'tensor', scatter_dimension=0, tiled=False)]
    gather x4 -> x1, local copies, waits for them, and re-layouts: 9.48 us -> 0.58 us  [per_device(): kv_scales[fork_export].reshape(1, -1)]
    slice x1 -> x0, local copies, waits for them, and re-layouts: 4.6 us -> none  [per_device(): far = every[:, :per * 2 * page].reshape(groups, per, 2, page, kv_cols)]
    unnamed x17 -> x19, local copies, waits for them, and re-layouts: 2.45 us -> 5.01 us
    gather x2 -> x3, local copies, waits for them, and re-layouts: 6.64 us -> 6.7 us  [per_device(): table = pool_ids[page_table]]
  transfers between devices with their start and end apart: 3 -> 3, of which waited for: 3 -> 1; matrix products, arithmetic and copies ran while one was open for 5% -> 6% of each run, Pallas kernels for 8% -> 50%
where the time goes in v2:
time: 236 us
  Pallas kernels  170 us (72%)
  waiting for transfers between devices  29.3 us (12%)
  local copies, waits for them, and re-layouts  18.5 us (8%)
  between operations  13.3 us (6%)
  other arithmetic  3.99 us (2%)
    pallas_call x1, Pallas kernels, per_device(): pl.pallas_call(functools.partial(exchange_kernel, far_count, near), out_s...  66.2 us
    pallas_call x2, Pallas kernels, per_device(): pl.pallas_call(functools.partial(attend_kernel, part * half_count, half_c...  65.8 us
    reduce_scatter x2, waiting for transfers between devices, per_device(): lax.psum_scatter(partial, 'tensor', scatter_dimension=0, tiled=False)  29.3 us
    pallas_call x1, Pallas kernels, per_device(): pl.pallas_call(project_kernel, out_shape=(jax.ShapeDtypeStruct((branches...  20.2 us
    pallas_call x1, Pallas kernels, per_device(): pl.pallas_call(offer_kernel, out_shape=jax.ShapeDtypeStruct((per * 2 * pa...  18 us
    gather x3, local copies, waits for them, and re-layouts, per_device(): table = pool_ids[page_table]  6.7 us
    unnamed x19, local copies, waits for them, and re-layouts  5.01 us
  transfers between devices with their start and end apart: 3, of which 1 were waited for; matrix products, arithmetic and copies ran while one was open for 6% of the time, Pallas kernels for 50%

profile of v2, /device:TPU:0, one launch (start us, length us, event | category | flops | bytes accessed | tf_op | source)
XLA Modules:
  0.0 235.7 jit_solution(5789672443023515905)
XLA Ops:
  6.5 0.0 copy-start
  6.5 0.0 all-gather.2.cloned.1.call-start
  6.5 2.1 all_gather_reshape.3
  8.7 0.0 all-gather.2.cloned.1.call-update
  8.7 0.0 reduce-scatter.3.cloned.1.call-start
  8.8 0.7 add_convert_fusion
  9.5 0.1 convert_element_type.29
  9.6 0.7 reshape.45.gain_ref
  10.3 0.7 compare_select_fusion
  11.0 0.1 copy.20
  11.1 0.1 reshape.52
  11.2 0.0 copy-done
  11.3 0.1 pad_add_fusion
  11.3 0.0 copy-start.7
  11.3 0.0 copy-start.8
  11.3 6.6 %gather_fusion = s32[1024]{0:T(1024)S(1)} fusion(s32[96]{0:T(128)S(1)} %pad_add_fusion, s32[1024]{0:T(1024)S(1)} %broadcast_clamp_fusion), kind=kCustom, calls=%fused_computation | custom fusion | bytes 12288 | tf_op jit(solution)/shard_map/gather | solution.py:302
  17.9 0.1 reshape.51
  18.1 0.0 copy-done.7
  18.1 0.1 copy.21
  18.2 0.0 copy-done.8
  18.2 0.6 gather_fusion.1
  18.8 0.1 reshape.46
  18.9 0.6 pad.8.tail_ref
  19.5 18.0 %shard_map.110.mine_ref = bf16[1040,256]{1,0:T(8,128)(2,1)} custom-call(s32[8]{0:T(128)} %export_ref.1, bf16[4096,256]{1,0:T(8,128)(2,1)} %bitcast.12, bf16[16,256]{1,0:T(8,128)(2,1)} %pad.8.tail_ref), custom_call_target="tpu_custom_call" | custom-call | tf_op jit(solution)/shard_map/pallas_call | solution.py:275
  37.5 66.2 %shard_map.111.far_ref = bf16[8,1040,256]{2,1,0:T(8,128)(2,1)} custom-call(bf16[1040,256]{1,0:T(8,128)(2,1)} %shard_map.110.mine_ref), custom_call_target="tpu_custom_call" | custom-call | bytes 157286400 | tf_op jit(solution)/shard_map/pallas_call | solution.py:283
  103.8 0.7 slice_reduce_fusion
  104.5 0.1 reshape_squeeze.3
  104.6 0.1 copy.22
  104.7 0.2 fusion
  104.9 0.2 copy.24
  105.1 1.0 fusion.2
  106.1 0.2 pad_maximum_fusion.1
  106.3 0.0 all-gather.2.cloned.1.call-done.hid_ref
  106.3 0.0 copy-start.1
  106.3 0.0 copy-start.4
  106.4 20.2 %shard_map.109 = (bf16[4096,128]{1,0:T(8,128)(2,1)S(1)}, bf16[512,256]{1,0:T(8,128)(2,1)S(1)}, bf16[512,256]{1,0:T(8,128)(2,1)S(1)}) custom-call(bf16[4,512,1024]{2,1,0:T(8,128)(2,1)} %all-gather.2.cloned.1.call-done.hid_ref, f32[4,1024]{1,0:T(4,128)S(1)} %reshape.45.gain_ref, f32[512,128]{1,0:T(8,128)S(1)} %get-tuple-element.14.cos_ref, ...), custom_call_target="tpu_custom_call" | custom-call | tf_op jit(solution)/shard_map/pallas_call | solution.py:311
  126.6 0.0 copy-done.1
  126.6 0.0 copy-done.4
  126.6 32.6 %shard_map.112 = bf16[4,256,1024]{2,1,0:T(8,128)(2,1)S(1)} custom-call(s32[1024]{0:T(1024)S(1)} %gather_fusion, s32[128]{0:T(128)S(1)} %copy-done.4, bf16[4096,128]{1,0:T(8,128)(2,1)S(1)} %get-tuple-element.8.q_ref, bf16[512,256]{1,0:T(8,128)(2,1)S(1)} %get-tuple-element.9.kn_ref, bf16[512,256]{1,0:T(8,128)(2,1)S(1)} %get-tuple-element.10.vn_ref, ...), custom_call_target="tpu_custom_call" | custom-call | flops 20000000000 | bytes 94371840 | tf_op jit(solution)/shard_map/pallas_call | solution.py:334
  159.2 0.0 copy-start.2
  159.2 1.3 copy-done.2
  160.6 0.0 copy-start.5
  160.6 1.0 copy-done.5
  161.5 0.0 reduce-scatter.3.cloned.1.call-update
  161.6 0.0 reduce-scatter.5.cloned.1.call-start
  161.6 0.0 copy-start.6
  161.6 1.2 copy-done.6
  162.8 33.2 %shard_map.113 = bf16[4,256,1024]{2,1,0:T(8,128)(2,1)S(1)} custom-call(s32[1024]{0:T(1024)S(1)} %gather_fusion, s32[128]{0:T(128)S(1)} %copy-done.4, bf16[4096,128]{1,0:T(8,128)(2,1)S(1)} %copy-done.6, bf16[512,256]{1,0:T(8,128)(2,1)S(1)} %get-tuple-element.9.kn_ref, bf16[512,256]{1,0:T(8,128)(2,1)S(1)} %get-tuple-element.10.vn_ref, ...), custom_call_target="tpu_custom_call" | custom-call | flops 20000000000 | bytes 94371840 | tf_op jit(solution)/shard_map/pallas_call | solution.py:334
  196.1 0.0 copy-start.3
  196.1 1.3 copy-done.3
  197.4 0.0 reduce-scatter.5.cloned.1.call-update
  197.4 0.0 reduce-scatter.3.cloned.1.call-done
  197.5 29.2 %reduce-scatter.5.cloned.1.call-done = bf16[1,256,1024]{2,1,0:T(8,128)(2,1)} async-done(((bf16[4,256,1024]{2,1,0:T(8,128)(2,1)}), bf16[1,256,1024]{2,1,0:T(8,128)(2,1)}) %reduce-scatter.5.cloned.1.call-update) | async-done | bytes 524304 | tf_op jit(solution)/shard_map/reduce_scatter | solution.py:353
  226.7 1.3 pad_maximum_fusion
  228.0 1.2 reshape.49
  (7 shorter events, 0.1 us)
Async XLA Ops:
  6.5 4.7 %copy-start = (s32[8,64]{1,0:T(8,128)S(1)}, s32[8,64]{1,0:T(8,128)}, u32[]{:S(2)}) copy-start(s32[8,64]{1,0:T(8,128)} %param.19) | copy-start | bytes 6148
  6.5 99.8 %all-gather.2.cloned.1.call-start = ((), (), s32[]{:S(2)}) async-start(), calls=%async_computation.2 | async-start | bytes 5242880 | tf_op jit(solution)/shard_map/all_gather | solution.py:254
  8.7 188.7 %reduce-scatter.3.cloned.1.call-start = ((), (), s32[]{:S(2)}) async-start(), calls=%async_computation.3 | async-start | bytes 2621440 | tf_op jit(solution)/shard_map/reduce_scatter | solution.py:353
  11.3 6.7 %copy-start.7 = (bf16[32,2,2]{0,2,1:T(2,128)(2,1)S(1)}, bf16[32,2,2]{0,2,1:T(2,128)(2,1)}, u32[]{:S(2)}) copy-start(bf16[32,2,2]{0,2,1:T(2,128)(2,1)} %param.17) | copy-start | bytes 772
  11.3 6.9 %copy-start.8 = (s32[8]{0:T(128)S(1)}, s32[8]{0:T(128)}, u32[]{:S(2)}) copy-start(s32[8]{0:T(128)} %export_ref.1) | copy-start | bytes 100
  106.3 20.2 %copy-start.1 = (bf16[32,2,64,256]{3,2,1,0:T(8,128)(2,1)S(1)}, bf16[32,2,64,256]{3,2,1,0:T(8,128)(2,1)}, u32[]{:S(2)}) copy-start(bf16[32,2,64,256]{3,2,1,0:T(8,128)(2,1)} %param.16) | copy-start | bytes 6291460
  106.3 20.2 %copy-start.4 = (s32[128]{0:T(128)S(1)}, s32[128]{0:T(128)}, u32[]{:S(2)}) copy-start(s32[128]{0:T(128)} %lens_ref.3) | copy-start | bytes 1540
  159.2 1.4 copy-start.2
  160.6 1.0 copy-start.5
  161.6 65.1 %reduce-scatter.5.cloned.1.call-start = ((), (), s32[]{:S(2)}) async-start(), calls=%async_computation.4 | async-start | bytes 2621440 | tf_op jit(solution)/shard_map/reduce_scatter | solution.py:353
  161.6 1.2 copy-start.6
  196.1 1.3 copy-start.3
Sparse Core Ops, SparseCore 0:
  8.9 37.1 all-gather.1
  161.7 29.6 reduce-scatter.2
  197.5 29.0 reduce-scatter.4
